TPU v7x, 32 devices: a whole 2x2x4 slice. The times are simulated.
32 devices in a mesh: fsdp: 8 (over z, y), slide: 4 (over x, core).
Axes of the slice: x: 2, y: 2, z: 4, core: 2. Of those that a mesh axis runs over, the one named last changes fastest.
Arguments:
- tiles: bfloat16 [16384, 1536], P(('slide', 'fsdp')), parts along dimension 0, may hold values from -6 to 6
- tile_cell: int32 [16384], P('slide'), parts along dimension 0, may hold values from 0 to 4095, as said below
- tissue: int32 [64, 256], P('slide'), parts along dimension 0, may hold values 0 or 1
- norm_gain: float32 [2, 1536], replicated, may hold values from 0.5 to 1.5
- qk_gain: float32 [2, 2, 64], replicated, may hold values from 0.5 to 4
- row_qkv: bfloat16 [1536, 4608], P(None, 'fsdp'), may hold values from -0.15625 to 0.15625
- row_out: bfloat16 [1536, 1536], P(None, 'fsdp'), may hold values from -0.15625 to 0.15625
- col_qkv: bfloat16 [1536, 4608], P(None, 'fsdp'), may hold values from -0.15625 to 0.15625
- col_out: bfloat16 [1536, 1536], P(None, 'fsdp'), may hold values from -0.15625 to 0.15625
Outputs:
- encoded: bfloat16 [64, 256, 1536], P('slide', 'fsdp'), parts along dimension 0
There are 4 independent parts, one for each index of `slide`. A program takes and returns all parts, laid end to end along the dimension named above; an argument that names none is the same for every part. Nothing has to cross between parts.
Inputs may be any that keep to these rules, and one draw needn't show every extreme that they name: Slots d * 512 + b * 64 up to d * 512 + (b + 1) * 64 - 1 hold tiles of grid rows b * 2 to (b + 1) * 2 - 1; tile_cell names every grid cell exactly once.
All inputs are finite; a program needn't handle non-finite values.
Results may differ from a plain program's by a relative error of at most 0.02.
The roundings to bfloat16 on the way count: a program that leaves them out, or rounds other values in their place, can miss the bound.
Values may be sent and summed in bfloat16 or wider, within the bound.
A program may use at most 256 MiB of HBM per device.

v0:
```python
import jax
import jax.numpy as jnp
from jax import lax
from jax.sharding import PartitionSpec as P

HEADS = 24


EPS = 1e-06


def rms_norm(grid, gain):
    values = grid.astype(jnp.float32)
    scale = lax.rsqrt(jnp.mean(values * values, axis=-1, keepdims=True) + EPS)
    return (values * scale * gain).astype(jnp.bfloat16)


def head_norm(values, gain):
    scale = lax.rsqrt(jnp.mean(values * values, axis=-1, keepdims=True) + EPS)
    return values * scale * gain


def rotate(values, rows_pos, cols_pos):
    quarter = values.shape[-1] // 4
    freq = 10000.0 ** (-jnp.arange(quarter).astype(jnp.float32) / quarter)

    def turn(part, position):
        angle = position.astype(jnp.float32)[..., None, None] * freq
        cosine = jnp.cos(angle)
        sine = jnp.sin(angle)
        first = part[..., :quarter]
        second = part[..., quarter:]
        return jnp.concatenate(
            [first * cosine - second * sine, first * sine + second * cosine], axis=-1
        )

    half = 2 * quarter
    return jnp.concatenate(
        [turn(values[..., :half], rows_pos), turn(values[..., half:], cols_pos)], axis=-1
    )


def attend(qkv, gains, rows_pos, cols_pos, keys_live, column, heads):
    width = qkv.shape[-1] // 3
    size = width // heads
    shape = qkv.shape[:-1] + (heads, size)
    query = qkv[..., :width].reshape(shape).astype(jnp.float32)
    key = qkv[..., width : 2 * width].reshape(shape).astype(jnp.float32)
    value = qkv[..., 2 * width :].reshape(shape)
    query = rotate(head_norm(query, gains[0]), rows_pos, cols_pos).astype(jnp.bfloat16)
    key = rotate(head_norm(key, gains[1]), rows_pos, cols_pos).astype(jnp.bfloat16)
    if column:
        score_form = "lbhd,mbhd->bhlm"
        mix_form = "bhlm,mbhd->lbhd"
        live = keys_live.T
    else:
        score_form = "blhd,bmhd->bhlm"
        mix_form = "bhlm,bmhd->blhd"
        live = keys_live
    scores = jnp.einsum(score_form, query, key, preferred_element_type=jnp.float32) * size ** (-0.5)
    length = scores.shape[-1]
    diagonal = jnp.arange(length)[:, None] == jnp.arange(length)[None, :]
    allow = (live[:, None, None, :] > 0) | diagonal[None, None]
    scores = jnp.where(allow, scores, -1e30)
    top = jnp.max(scores, axis=-1, keepdims=True)
    weights = jnp.exp(scores - top)
    total = jnp.sum(weights, axis=-1)
    mixed = jnp.einsum(
        mix_form, weights.astype(jnp.bfloat16), value, preferred_element_type=jnp.float32
    )
    if column:
        total = total.transpose(2, 0, 1)
    else:
        total = total.transpose(0, 2, 1)
    return (mixed / total[..., None]).reshape(qkv.shape[:-1] + (width,)).astype(jnp.bfloat16)


def project_qkv(normed, weight):

    def multiply(piece, start):
        return jnp.dot(normed, piece, preferred_element_type=jnp.float32)

    return multiply(lax.all_gather(weight, "fsdp", axis=1, tiled=True), jnp.int32(0)).astype(
        jnp.bfloat16
    )


def project_out(mixed, weight):

    def multiply(piece, start):
        return jnp.dot(mixed, piece, preferred_element_type=jnp.float32)

    return multiply(lax.all_gather(weight, "fsdp", axis=1, tiled=True), jnp.int32(0))


def on_device(tiles, tile_cell, tissue, norm_gain, qk_gain, row_qkv, row_out, col_qkv, col_out):
    count = lax.axis_size("fsdp")
    index = lax.axis_index("fsdp")
    width = tiles.shape[1]
    tok_dev = tiles.shape[0]
    slots = tok_dev // count
    grid_rows = tissue.shape[0]
    columns = tissue.shape[1]
    rows_dev = grid_rows // count
    cols_dev = columns // count
    arrived = lax.all_to_all(
        tiles.reshape(count, slots, width), "fsdp", split_axis=0, concat_axis=0, tiled=True
    )
    table_cell = lax.dynamic_index_in_dim(
        tile_cell.reshape(count, count, slots), index, 1, keepdims=False
    )
    row_base = index * rows_dev
    local_cells = (table_cell - row_base * columns).reshape(-1)
    grid = (
        jnp.zeros((tok_dev, width), jnp.bfloat16)
        .at[local_cells]
        .set(arrived.reshape(tok_dev, width))
    )
    rows_pos = row_base + lax.broadcasted_iota(jnp.int32, (rows_dev, columns), 0)
    cols_pos = lax.broadcasted_iota(jnp.int32, (rows_dev, columns), 1)
    live_rows = lax.dynamic_slice_in_dim(tissue, row_base, rows_dev, 0)
    qkv = project_qkv(rms_norm(grid, norm_gain[0]), row_qkv).reshape(rows_dev, columns, 3 * width)
    mixed = attend(qkv, qk_gain[0], rows_pos, cols_pos, live_rows, False, HEADS)
    hidden = grid.astype(jnp.float32) + project_out(mixed.reshape(tok_dev, width), row_out)
    hidden = hidden.astype(jnp.bfloat16).reshape(rows_dev, columns, width)
    turned = lax.all_to_all(hidden, "fsdp", split_axis=1, concat_axis=0, tiled=True)
    col_base = index * cols_dev
    rows_pos_col = lax.broadcasted_iota(jnp.int32, (grid_rows, cols_dev), 0)
    cols_pos_col = col_base + lax.broadcasted_iota(jnp.int32, (grid_rows, cols_dev), 1)
    live_cols = lax.dynamic_slice_in_dim(tissue, col_base, cols_dev, 1)
    flat = turned.reshape(grid_rows * cols_dev, width)
    qkv_col = project_qkv(rms_norm(flat, norm_gain[1]), col_qkv).reshape(
        grid_rows, cols_dev, 3 * width
    )
    mixed_col = attend(qkv_col, qk_gain[1], rows_pos_col, cols_pos_col, live_cols, True, HEADS)
    result = flat.astype(jnp.float32) + project_out(
        mixed_col.reshape(grid_rows * cols_dev, width), col_out
    )
    return result.astype(jnp.bfloat16).reshape(grid_rows, cols_dev, width)


def solution(mesh):
    return jax.shard_map(
        on_device,
        mesh=mesh,
        in_specs=(
            P(("slide", "fsdp"), None),
            P("slide"),
            P("slide", None),
            P(),
            P(),
            P(None, "fsdp"),
            P(None, "fsdp"),
            P(None, "fsdp"),
            P(None, "fsdp"),
        ),
        out_specs=P("slide", "fsdp", None),
        check_vma=False,
    )
```

profile of v0, /device:TPU:0, one launch (start us, length us, event | category | flops | bytes accessed | tf_op | source)
XLA Modules:
  0.0 659.5 jit_solution(4190101427166727166)
XLA Ops:
  6.5 0.7 all-gather.5.cloned.1.call-update
  7.3 0.7 all-gather.7.cloned.1.call-update
  8.1 0.7 all-gather.9.cloned.1.call-update
  8.8 7.3 %all-to-all-start = ((bf16[8,64,1536]{2,1,0:T(8,128)(2,1)}), bf16[8,64,1536]{2,1,0:T(8,128)(2,1)S(1)}, u32[]{:S(2)}, u32[]{:S(2)}) async-start(bf16[8,64,1536]{2,1,0:T(8,128)(2,1)} %bitcast.1), calls=%async_computation | async-start | bytes 3145728 | tf_op jit(solution)/shard_map/all_to_all | solution.py:106
  16.2 0.1 sub.59
  16.4 0.2 multiply_cosine_fusion.3
  16.6 0.1 broadcast_or_fusion
  16.8 70.5 %all-to-all-done = bf16[8,64,1536]{2,1,0:T(8,128)(2,1)S(1)} async-done(((bf16[8,64,1536]{2,1,0:T(8,128)(2,1)}), bf16[8,64,1536]{2,1,0:T(8,128)(2,1)S(1)}, u32[]{:S(2)}, u32[]{:S(2)}) %all-to-all-start) | async-done | bytes 1572896 | tf_op jit(solution)/shard_map/all_to_all | solution.py:106
  87.3 3.4 scatter_custom_fusion
  90.8 0.4 fusion.15
  91.2 143.6 %all-gather.5.cloned.1.call-done = bf16[1536,4608]{0,1:T(8,128)(2,1)} async-done(((bf16[1536,576]{0,1:T(8,128)(2,1)}), bf16[1536,4608]{0,1:T(8,128)(2,1)}) %all-gather.5.cloned.1.call-update) | async-done | bytes 14155792 | tf_op jit(solution)/shard_map/all_gather | solution.py:83
  234.7 11.5 %convolution_convert_fusion.1 = bf16[512,4608]{1,0:T(8,128)(2,1)S(1)} fusion(bf16[1536,4608]{0,1:T(8,128)(2,1)} %all-gather.5.cloned.1.call-done, bf16[512,1536]{1,0:T(8,128)(2,1)S(1)} %scatter_custom_fusion, f32[1536]{0:T(1024)S(1)} %get-tuple-element.6, f32[512]{0:T(512)S(1)} %add_rsqrt_fusion.5), kind=kOutput, calls=%fused_computation.7 | convolution fusion | flops 7253262336 | bytes 20455424 | tf_op jit(solution)/shard_map/dot_general | solution.py:81
  246.2 3.1 slice_convert_fusion.2
  249.3 2.3 copy.76
  251.6 2.4 copy.77
  254.0 2.6 copy.75
  256.6 2.5 multiply_reduce_fusion.4
  259.1 0.4 multiply_reduce_fusion.3
  259.6 0.7 multiply_multiply_fusion.1
  260.2 0.5 subtract_convert_fusion.7
  260.8 0.5 multiply_multiply_fusion
  261.3 0.5 subtract_convert_fusion.5
  261.9 2.4 fusion
  264.3 3.1 fusion.1
  267.4 3.4 fusion.37
  270.9 1.6 copy.79
  272.5 0.3 copy.96
  272.8 42.2 %all-gather.7.cloned.1.call-done = bf16[1536,1536]{0,1:T(8,128)(2,1)} async-done(((bf16[1536,192]{0,1:T(8,128)(2,1)}), bf16[1536,1536]{0,1:T(8,128)(2,1)}) %all-gather.7.cloned.1.call-update) | async-done | bytes 4718608 | tf_op jit(solution)/shard_map/all_gather | solution.py:93
  315.0 5.0 fusion.44
  320.0 2.8 copy.80
  322.8 3.6 all-to-all-start.1
  326.4 0.5 all-gather.11.cloned.1.call-update
  327.0 0.1 fusion.71
  327.1 0.1 copy.84
  327.2 0.1 broadcast_or_fusion.1
  327.3 2.3 multiply_cosine_fusion.1
  329.6 76.4 %all-to-all-done.1 = bf16[2,256,1536]{2,0,1:T(2,128)(2,1)S(1)} async-done(((bf16[2,256,1536]{2,0,1:T(2,128)(2,1)}), bf16[2,256,1536]{2,0,1:T(2,128)(2,1)S(1)}, u32[]{:S(2)}, u32[]{:S(2)}) %all-to-all-start.1) | async-done | bytes 1572896 | tf_op jit(solution)/shard_map/all_to_all | solution.py:126
  406.0 2.1 copy.81
  408.1 1.7 multiply_reduce_fusion.2
  409.8 0.1 copy.83
  410.0 0.1 rsqrt.55
  410.0 2.2 fusion.36
  412.3 131.8 %all-gather.9.cloned.1.call-done = bf16[1536,4608]{0,1:T(8,128)(2,1)} async-done(((bf16[1536,576]{0,1:T(8,128)(2,1)}), bf16[1536,4608]{0,1:T(8,128)(2,1)}) %all-gather.9.cloned.1.call-update) | async-done | bytes 14155792 | tf_op jit(solution)/shard_map/all_gather | solution.py:83
  544.1 10.7 %convolution_convert_fusion = bf16[512,4608]{1,0:T(8,128)(2,1)S(1)} fusion(bf16[512,1536]{1,0:T(8,128)(2,1)S(1)} %fusion.36, bf16[1536,4608]{0,1:T(8,128)(2,1)} %all-gather.9.cloned.1.call-done), kind=kOutput, calls=%fused_computation.6 | convolution fusion | flops 7250116608 | bytes 20447232 | tf_op jit(solution)/shard_map/dot_general | solution.py:81
  554.9 3.2 fusion.78
  558.0 5.5 reshape.256
  563.5 5.2 multiply_reduce_fusion.1
  568.7 1.8 copy.85
  570.5 1.6 add_rsqrt_fusion.1
  572.1 1.9 copy.86
  574.0 3.5 reshape.257
  577.5 4.7 multiply_reduce_fusion
  582.2 0.1 copy.88
  582.4 0.2 copy.89
  582.6 3.2 reshape.249
  585.8 12.0 %fusion.6 = (f32[16,32,24,64]{3,0,2,1:T(8,128)S(1)}, f32[16,32,24,64]{3,0,2,1:T(8,128)S(1)}) fusion(f32[16,32,24,64]{3,2,1,0:T(8,128)} %reshape.257, f32[64]{0:T(128)S(1)} %get-tuple-element.37, f32[16,32,24]{0,2,1:T(8,128)S(1)} %copy.89, f32[64]{0:T(128)S(1)} %get-tuple-element.40, f32[16,32,24]{0,2,1:T(8,128)S(1)} %copy-done.12, ...), kind=kLoop, calls=%fused_computation.12 | loop fusion | flops 3145728 | bytes 12681728 | tf_op jit(solution)/shard_map/mul | solution.py:20
  597.8 8.1 %subtract_convert_fusion.3 = (bf16[16,32,24,16]{3,0,2,1:T(8,128)(2,1)}, bf16[16,32,24,16]{3,0,2,1:T(8,128)(2,1)}, bf16[16,32,24,16]{3,0,2,1:T(8,128)(2,1)}, bf16[16,32,24,16]{3,0,2,1:T(8,128)(2,1)}) fusion(f32[16,32,24,64]{3,0,2,1:T(8,128)S(1)} %get-tuple-element.58, f32[16,32,16]{2,0,1:T(8,128)S(1)} %copy-done.8, f32[16,32,16]{2,0,1:T(8,128)S(1)} %get-tuple-element.43, ...), kind=kLoop, calls=%fused_computation.25 | loop fusion | flops 3145728 | bytes 4849664 | tf_op jit(solution)/shard_map/convert.11
  606.0 7.7 %subtract_convert_fusion.1 = (bf16[16,32,24,16]{3,0,2,1:T(8,128)(2,1)}, bf16[16,32,24,16]{3,0,2,1:T(8,128)(2,1)}, bf16[16,32,24,16]{3,0,2,1:T(8,128)(2,1)}, bf16[16,32,24,16]{3,0,2,1:T(8,128)(2,1)}) fusion(f32[16,32,24,64]{3,0,2,1:T(8,128)S(1)} %get-tuple-element.57, f32[16,32,16]{2,0,1:T(8,128)S(1)} %copy-done.8, f32[16,32,16]{2,0,1:T(8,128)S(1)} %get-tuple-element.43, ...), kind=kLoop, calls=%fused_computation.20 | loop fusion | flops 3145728 | bytes 4849664 | tf_op jit(solution)/shard_map/convert.7
  613.7 13.3 %fusion.12 = (f32[32,24,16]{2,1,0:T(8,128)S(1)}, f32[32,24,16,16]{2,3,1,0:T(8,128)S(1)}) fusion(pred[32,16,16]{1,2,0:T(8,128)(4,1)S(1)} %broadcast_or_fusion.1, bf16[16,32,24,16]{3,0,2,1:T(8,128)(2,1)} %get-tuple-element.15, bf16[16,32,24,16]{3,0,2,1:T(8,128)(2,1)} %get-tuple-element.16, bf16[16,32,24,16]{3,0,2,1:T(8,128)(2,1)} %get-tuple-element.8, ...), kind=kOutput, calls=%fused_computation.31 | convolution fusion | flops 38326272 | bytes 3989504 | tf_op jit(solution)/shard_map/lbhd,mbhd->bhlm/dot_general | solution.py:60
  627.0 2.7 fusion.13
  629.7 8.5 %fusion.5 = bf16[16,32,24,64]{3,0,2,1:T(8,128)(2,1)S(1)} fusion(f32[16,32,24]{0,2,1:T(8,128)S(1)} %bitcast.73, f32[32,24,16,16]{2,3,1,0:T(8,128)S(1)} %get-tuple-element.56, f32[32,24,16]{2,1,0:T(8,128)S(1)} %get-tuple-element.55, pred[32,16,16]{1,2,0:T(8,128)(4,1)S(1)} %broadcast_or_fusion.1, bf16[16,32,24,64]{3,2,1,0:T(8,128)(2,1)S(1)} %copy-done.7), kind=kOutput, calls=%fused_computation.10 | convolution fusion | flops 27525120 | bytes 4038656 | tf_op jit(solution)/shard_map/bhlm,mbhd->lbhd/dot_general | solution.py:68
  638.2 2.5 copy.93
  640.7 5.5 convert_element_type.194
  646.2 6.6 fusion.43
  (57 shorter events, 0.5 us)
Async XLA Ops:
  6.5 228.2 %all-gather.5.cloned.1.call-start = ((), (), s32[]{:S(2)}) async-start(), calls=%async_computation.2 | async-start | bytes 15925248 | tf_op jit(solution)/shard_map/all_gather | solution.py:83
  7.3 8.8 %copy-start.13 = (s32[4096]{0:T(1024)S(1)}, s32[4096]{0:T(1024)}, u32[]{:S(2)}) copy-start(s32[4096]{0:T(1024)} %param.10) | copy-start | bytes 49156
  7.3 9.0 %copy-start.15 = (s32[16,256]{1,0:T(8,128)S(1)}, s32[16,256]{1,0:T(8,128)}, u32[]{:S(2)}) copy-start(s32[16,256]{1,0:T(8,128)} %param.11) | copy-start | bytes 49156
  7.3 9.1 %copy-start.14 = (f32[2,1536]{1,0:T(2,128)S(1)}, f32[2,1536]{1,0:T(2,128)}, u32[]{:S(2)}) copy-start(f32[2,1536]{1,0:T(2,128)} %param.12) | copy-start | bytes 36868
  7.3 9.1 %copy-start.16 = (f32[2,2,64]{2,1,0:T(2,128)S(1)}, f32[2,2,64]{2,1,0:T(2,128)}, u32[]{:S(2)}) copy-start(f32[2,2,64]{2,1,0:T(2,128)} %param.13) | copy-start | bytes 3076
  7.3 307.7 %all-gather.7.cloned.1.call-start = ((), (), s32[]{:S(2)}) async-start(), calls=%async_computation.3 | async-start | bytes 5308416 | tf_op jit(solution)/shard_map/all_gather | solution.py:93
  8.0 536.1 %all-gather.9.cloned.1.call-start = ((), (), s32[]{:S(2)}) async-start(), calls=%async_computation.4 | async-start | bytes 15925248 | tf_op jit(solution)/shard_map/all_gather | solution.py:83
  8.8 78.6 %all-to-all-start = ((bf16[8,64,1536]{2,1,0:T(8,128)(2,1)}), bf16[8,64,1536]{2,1,0:T(8,128)(2,1)S(1)}, u32[]{:S(2)}, u32[]{:S(2)}) async-start(bf16[8,64,1536]{2,1,0:T(8,128)(2,1)} %bitcast.1), calls=%async_computation | async-start | bytes 3145728 | tf_op jit(solution)/shard_map/all_to_all | solution.py:106
  90.8 155.4 %copy-start.4 = (bf16[512,1536]{1,0:T(8,128)(2,1)}, bf16[512,1536]{1,0:T(8,128)(2,1)S(1)}, u32[]{:S(2)}) copy-start(bf16[512,1536]{1,0:T(8,128)(2,1)S(1)} %scatter_custom_fusion) | copy-start | bytes 4718596
  256.6 3.0 copy-start
  264.3 3.1 copy-start.11
  270.9 44.2 %copy-start.5 = (bf16[512,1536]{1,0:T(8,128)(2,1)S(1)}, bf16[512,1536]{1,0:T(8,128)(2,1)}, u32[]{:S(2)}) copy-start(bf16[512,1536]{1,0:T(8,128)(2,1)} %copy-done.4) | copy-start | bytes 4718596
  322.8 83.2 %all-to-all-start.1 = ((bf16[2,256,1536]{2,0,1:T(2,128)(2,1)}), bf16[2,256,1536]{2,0,1:T(2,128)(2,1)S(1)}, u32[]{:S(2)}, u32[]{:S(2)}) async-start(bf16[2,256,1536]{2,0,1:T(2,128)(2,1)} %copy.80), calls=%async_computation.1 | async-start | bytes 3145728 | tf_op jit(solution)/shard_map/all_to_all | solution.py:126
  326.4 319.8 %all-gather.11.cloned.1.call-start = ((), (), s32[]{:S(2)}) async-start(), calls=%async_computation.5 | async-start | bytes 5308416 | tf_op jit(solution)/shard_map/all_gather | solution.py:93
  577.5 5.1 copy-start.6
  582.2 3.6 copy-start.12
  585.8 12.0 %copy-start.8 = (f32[16,32,16]{2,0,1:T(8,128)S(1)}, f32[16,32,16]{2,0,1:T(8,128)}, u32[]{:S(2)}) copy-start(f32[16,32,16]{2,0,1:T(8,128)} %get-tuple-element.44) | copy-start | bytes 98308
  585.8 12.0 %copy-start.9 = (f32[16,32,16]{2,0,1:T(8,128)S(1)}, f32[16,32,16]{2,0,1:T(8,128)}, u32[]{:S(2)}) copy-start(f32[16,32,16]{2,0,1:T(8,128)} %get-tuple-element.49) | copy-start | bytes 98308
  585.8 12.0 %copy-start.10 = (f32[16,32,16]{2,0,1:T(8,128)S(1)}, f32[16,32,16]{2,0,1:T(8,128)}, u32[]{:S(2)}) copy-start(f32[16,32,16]{2,0,1:T(8,128)} %get-tuple-element.50) | copy-start | bytes 98308
  606.0 7.7 %copy-start.2 = (bf16[16,32,24,16]{3,0,2,1:T(8,128)(2,1)S(1)}, bf16[16,32,24,16]{3,0,2,1:T(8,128)(2,1)}, u32[]{:S(2)}) copy-start(bf16[16,32,24,16]{3,0,2,1:T(8,128)(2,1)} %get-tuple-element.11) | copy-start | bytes 1179652
  606.0 7.7 %copy-start.3 = (bf16[16,32,24,16]{3,0,2,1:T(8,128)(2,1)S(1)}, bf16[16,32,24,16]{3,0,2,1:T(8,128)(2,1)}, u32[]{:S(2)}) copy-start(bf16[16,32,24,16]{3,0,2,1:T(8,128)(2,1)} %get-tuple-element.12) | copy-start | bytes 1179652
  627.0 2.7 copy-start.7
  640.7 5.5 copy-start.1
Sparse Core Ops, SparseCore 0:
  9.5 225.1 all-gather.4
  236.9 78.0 all-gather.6
  317.2 226.8 all-gather.8
  546.1 78.0 all-gather.10
where the time goes:
time: 664 us; the launch traced here: 660 us
  waiting for transfers between devices  467 us (70%)
  other arithmetic  63.9 us (10%)
  matrix products  61.4 us (9%)
  local copies, waits for them, and re-layouts  42.2 us (6%)
  between operations  13.8 us (2%)
  starting transfers between devices  11 us (2%)
    all_gather x2, waiting for transfers between devices, project_qkv(): lax.all_gather(weight, 'fsdp', axis=1, tiled=True)  275 us
    all_to_all x1, waiting for transfers between devices, on_device(): lax.all_to_all(hidden, 'fsdp', split_axis=1, concat_axis=0, tiled=True)  76.4 us
    all_to_all x1, waiting for transfers between devices, on_device(): lax.all_to_all(tiles.reshape(count, slots, width), 'fsdp', split_axis=0,...  70.5 us
    all_gather x2, waiting for transfers between devices, project_out(): lax.all_gather(weight, 'fsdp', axis=1, tiled=True)  42.2 us
    dot_general x2, matrix products, multiply(): return jnp.dot(normed, piece, preferred_element_type=jnp.float32)  22.2 us
    another operation x4, other arithmetic  16.9 us
    dot_general x2, matrix products, attend(): jnp.einsum(score_form, query, key, preferred_element_type=jnp.float32)  15.7 us
  transfers between devices with their start and end apart: 6, of which 5 were waited for; matrix products, arithmetic and copies ran while one was open for 24% of the time, Pallas kernels for 0%

commit v1 on v0

--- a/solution.py
+++ b/solution.py
@@ -1,9 +1,14 @@
+import functools
+
 import jax
 import jax.numpy as jnp
 from jax import lax
+from jax.experimental import pallas as pl
+from jax.experimental.pallas import tpu as pltpu
 from jax.sharding import PartitionSpec as P
 
 HEADS = 24
+MESH = pl.DeviceIdType.MESH
 
 
 EPS = 1e-06
@@ -76,6 +81,8 @@
 
 
 def project_qkv(normed, weight):
+    if weight.ndim == 3:
+        return stacked(normed, weight).astype(jnp.bfloat16)
 
     def multiply(piece, start):
         return jnp.dot(normed, piece, preferred_element_type=jnp.float32)
@@ -86,11 +93,119 @@
 
 
 def project_out(mixed, weight):
+    if weight.ndim == 3:
+        return stacked(mixed, weight)
 
     def multiply(piece, start):
         return jnp.dot(mixed, piece, preferred_element_type=jnp.float32)
 
     return multiply(lax.all_gather(weight, "fsdp", axis=1, tiled=True), jnp.int32(0))
+
+
+def gather_kernel(n, part, *refs):
+    ws, outs = refs[:n], refs[n:2*n]
+    loc, send, zr, yr, xr, cr = refs[2*n:]
+    s, f = lax.axis_index("slide"), lax.axis_index("fsdp")
+    x, c, z, y = s // 2, s % 2, f // 2, f % 2
+    zdev = lambda d: (lax.rem(z + d, 4) * 2 + y, s)
+    ydev = (z * 2 + 1 - y, s)
+    xdev = (f, (1 - x) * 2 + c)
+    cdev = (f, x * 2 + 1 - c)
+    bar = pltpu.get_barrier_semaphore()
+    peers = [zdev(1), zdev(2), zdev(3), ydev, xdev, cdev]
+    for p in peers:
+        pl.semaphore_signal(bar, inc=1, device_id=p, device_id_type=MESH)
+    pl.semaphore_wait(bar, len(peers))
+    sends = []
+    rows = ws[0].shape[0]
+    rest = (rows - 4 * part) // 2
+    def span(k, ax, ac):
+        if k == 0:
+            return pl.ds(pl.multiple_of((ax * 2 + ac) * part, 16), part)
+        return pl.ds(pl.multiple_of(4 * part + ac * rest, 16), rest)
+    kinds = (0, 1) if rest else (0,)
+    count = [0] * n
+    def push(a, src, fsrc, sp, dev, rsem):
+        cp = pltpu.make_async_remote_copy(src_ref=src, dst_ref=outs[a].at[fsrc, sp], send_sem=send.at[a, count[a]],
+            recv_sem=rsem, device_id=dev, device_id_type=MESH)
+        count[a] += 1
+        cp.start()
+        sends.append(cp)
+    def arrived(a, fsrc, sp, rsem):
+        r = outs[a].at[fsrc, sp]
+        pltpu.make_async_remote_copy(src_ref=r, dst_ref=r, send_sem=send.at[a, 0], recv_sem=rsem, device_id=cdev, device_id_type=MESH).wait_recv()
+    local = []
+    for a in range(n):
+        for k in kinds:
+            sp = span(k, x, c)
+            for d in (1, 3, 2):
+                push(a, ws[a].at[sp], f, sp, zdev(d), zr.at[a, k, d - 1])
+            push(a, ws[a].at[sp], f, sp, ydev, yr.at[a, k, 0])
+        cp = pltpu.make_async_copy(ws[a], outs[a].at[f], loc.at[a])
+        cp.start()
+        local.append(cp)
+    zf = lambda d: lax.rem(z - d + 4, 4) * 2 + y
+    yf = lambda d: lax.rem(z - d + 4, 4) * 2 + 1 - y
+    def stage_z(a):
+        for d in (1, 3, 2):
+            fs = zf(d)
+            for k in kinds:
+                sp = span(k, x, c)
+                arrived(a, fs, sp, zr.at[a, k, d - 1])
+                o = outs[a].at[fs, sp]
+                push(a, o, fs, sp, ydev, yr.at[a, k, d])
+                if k == 0:
+                    push(a, o, fs, sp, xdev, xr.at[a, d - 1])
+                push(a, o, fs, sp, cdev, cr.at[a, k, d - 1])
+    def stage_y(a):
+        for d in (0, 1, 3, 2):
+            fs = yf(d)
+            for k in kinds:
+                sp = span(k, x, c)
+                arrived(a, fs, sp, yr.at[a, k, d])
+                o = outs[a].at[fs, sp]
+                if k == 0:
+                    push(a, o, fs, sp, xdev, xr.at[a, 3 + d])
+                push(a, o, fs, sp, cdev, cr.at[a, k, 3 + d])
+    order = [(zf(d), d - 1) for d in (1, 3, 2)] + [(yf(d), 3 + d) for d in (0, 1, 3, 2)]
+    def stage_x(a):
+        for fs, i in order:
+            sp = span(0, 1 - x, c)
+            arrived(a, fs, sp, xr.at[a, i])
+            push(a, outs[a].at[fs, sp], fs, sp, cdev, cr.at[a, 2, i])
+    for a in range(n):
+        stage_z(a)
+        stage_y(a)
+        stage_x(a)
+    for a in range(n):
+        for fs, i in order:
+            for k, sp in ((0, span(0, x, 1 - c)), (1, span(1, x, 1 - c)), (2, span(0, 1 - x, 1 - c))):
+                if k == 1 and not rest: continue
+                arrived(a, fs, sp, cr.at[a, k, i])
+        local[a].wait()
+    for cp in sends:
+        cp.wait_send()
+
+def gather(*ws):
+    n = len(ws)
+    part = ws[0].shape[0] * 3 // 16
+    D = pltpu.SemaphoreType.DMA
+    return pl.pallas_call(functools.partial(gather_kernel, n, part),
+        out_shape=[jax.ShapeDtypeStruct((8,) + w.shape, w.dtype) for w in ws],
+        in_specs=[pl.BlockSpec(memory_space=pl.ANY)] * n,
+        out_specs=[pl.BlockSpec(memory_space=pl.ANY)] * n,
+        scratch_shapes=[D((n,)), D((n, 42)), D((n, 2, 3)), D((n, 2, 4)), D((n, 7)), D((n, 3, 7))],
+        compiler_params=pltpu.CompilerParams(collective_id=0, has_side_effects=True),
+        name="gather")(*ws)
+
+
+def fits(count, width):
+    return count == 8 and lax.axis_size("slide") == 4 and width % 256 == 0
+
+
+def stacked(values, weight):
+    out = jnp.einsum("tk,fkn->ftn", values, weight, preferred_element_type=jnp.float32)
+    return out.astype(jnp.float32).transpose(1, 0, 2).reshape(values.shape[0], -1)
 
 
 def on_device(tiles, tile_cell, tissue, norm_gain, qk_gain, row_qkv, row_out, col_qkv, col_out):
@@ -99,6 +214,8 @@
     width = tiles.shape[1]
     tok_dev = tiles.shape[0]
     slots = tok_dev // count
+    if fits(count, width):
+        row_qkv, row_out, col_qkv, col_out = gather(row_qkv, row_out, col_qkv, col_out)
     grid_rows = tissue.shape[0]
     columns = tissue.shape[1]
     rows_dev = grid_rows // count

time: 664 us -> 518 us (0.78)
  waiting for transfers between devices: 467 us -> 8.41 us
  Pallas kernels: 0 us -> 258 us
  local copies, waits for them, and re-layouts: 42.2 us -> 108 us
  between operations: 13.8 us -> 0.96 us
    all_gather x4 -> x0, waiting for transfers between devices: 318 us -> none  [the longest x2 275 us: project_qkv(): lax.all_gather(weight, 'fsdp', axis=1, tiled=True)]
    pallas_call x0 -> x1, Pallas kernels: none -> 258 us  [gather(): pl.pallas_call(functools.partial(gather_kernel, n, part), out_shape=[jax....]
    all_to_all x1, waiting for transfers between devices: 70.5 us -> 0.01 us  [on_device(): lax.all_to_all(tiles.reshape(count, slots, width), 'fsdp', split_axis=0,...]
    all_to_all x1, waiting for transfers between devices: 76.4 us -> 8.41 us  [on_device(): lax.all_to_all(hidden, 'fsdp', split_axis=1, concat_axis=0, tiled=True)]
    dot_general x0 -> x3, local copies, waits for them, and re-layouts: none -> 35 us  [stacked(): jnp.einsum('tk,fkn->ftn', values, weight, preferred_element_type=jnp.floa...]
    unnamed x35 -> x47, local copies, waits for them, and re-layouts: 0.4 us -> 20.2 us
    convert_element_type x0 -> x1, local copies, waits for them, and re-layouts: none -> 7.69 us  [project_qkv(): return stacked(normed, weight).astype(jnp.bfloat16)]
  transfers between devices with their start and end apart: 6 -> 2, of which waited for: 5 -> 1; matrix products, arithmetic and copies ran while one was open for 24% -> 9% of each run, Pallas kernels for 0% -> 50%
where the time goes in v1:
time: 518 us; the launch traced here: 511 us
  Pallas kernels  258 us (50%)
  local copies, waits for them, and re-layouts  108 us (21%)
  matrix products  61.3 us (12%)
  other arithmetic  60.7 us (12%)
  starting transfers between devices  13.7 us (3%)
  waiting for transfers between devices  8.41 us (2%)
    pallas_call x1, Pallas kernels, gather(): pl.pallas_call(functools.partial(gather_kernel, n, part), out_shape=[jax....  258 us
    dot_general x3, local copies, waits for them, and re-layouts, stacked(): jnp.einsum('tk,fkn->ftn', values, weight, preferred_element_type=jnp.floa...  35 us
    dot_general x4, matrix products, stacked(): jnp.einsum('tk,fkn->ftn', values, weight, preferred_element_type=jnp.floa...  32.9 us
    unnamed x47, local copies, waits for them, and re-layouts  20.2 us
    another operation x4, other arithmetic  16.8 us
    dot_general x2, matrix products, attend(): jnp.einsum(score_form, query, key, preferred_element_type=jnp.float32)  16.7 us
    mul x3, other arithmetic, head_norm(): return values * scale * gain  13.1 us
    reduce_sum x4, other arithmetic, head_norm(): scale = lax.rsqrt(jnp.mean(values * values, axis=-1, keepdims=True) + EPS)  12.5 us
  transfers between devices with their start and end apart: 2, of which 1 were waited for; matrix products, arithmetic and copies ran while one was open for 9% of the time, Pallas kernels for 50%

profile of v1, /device:TPU:0, one launch (start us, length us, event | category | flops | bytes accessed | tf_op | source)
XLA Modules:
  0.0 510.8 jit_solution(15815615677033895004)
XLA Ops:
  0.0 7.4 %all-to-all-start = ((bf16[8,64,1536]{2,1,0:T(8,128)(2,1)}), bf16[8,64,1536]{2,1,0:T(8,128)(2,1)}, u32[]{:S(2)}, u32[]{:S(2)}) async-start(bf16[8,64,1536]{2,1,0:T(8,128)(2,1)} %bitcast.86), calls=%async_computation | async-start | bytes 3145728 | tf_op jit(solution)/shard_map/all_to_all | solution.py:223
  7.4 2.3 copy.91.refs_0_
  9.7 2.3 copy.92.refs_1_
  12.0 2.3 copy.93.refs_2_
  14.3 1.2 copy.94.refs_3_
  15.6 257.6 %gather.1 = (bf16[8,1536,576]{2,1,0:T(8,128)(2,1)}, bf16[8,1536,192]{2,1,0:T(8,128)(2,1)}, bf16[8,1536,576]{2,1,0:T(8,128)(2,1)}, bf16[8,1536,192]{2,1,0:T(8,128)(2,1)}) custom-call(bf16[1536,576]{1,0:T(8,128)(2,1)} %copy.91.refs_0_, bf16[1536,192]{1,0:T(8,128)(2,1)} %copy.92.refs_1_, bf16[1536,576]{1,0:T(8,128)(2,1)} %copy.93.refs_2_, ...), custom_call_target="tpu_custom_call" | custom-call | tf_op jit(solution)/shard_map/gather/pallas_call | solution.py:193
  273.3 8.0 %copy.103 = bf16[8,192,1536]{2,1,0:T(8,128)(2,1)} copy(bf16[8,192,1536]{1,2,0:T(8,128)(2,1)} %bitcast.79) | data formatting | bytes 9437184 | tf_op jit(solution)/shard_map/tk,fkn->ftn/dot_general | solution.py:207
  281.5 0.2 multiply_cosine_fusion.3
  281.7 0.1 broadcast_or_fusion
  281.8 4.5 scatter_custom_fusion
  286.3 0.4 fusion.15
  286.7 13.5 %convolution_convert_fusion.1 = bf16[512,8,576]{0,2,1:T(8,128)(2,1)} fusion(bf16[8,1536,576]{2,1,0:T(8,128)(2,1)} %get-tuple-element.9, bf16[512,1536]{1,0:T(8,128)(2,1)S(1)} %scatter_custom_fusion, f32[1536]{0:T(1024)S(1)} %get-tuple-element.14, f32[512]{0:T(512)S(1)} %add_rsqrt_fusion.5), kind=kOutput, calls=%fused_computation.74 | convolution fusion | flops 7253262336 | bytes 20455424 | tf_op jit(solution)/shard_map/tk,fkn->ftn/dot_general | solution.py:207
  300.3 7.7 %convert_element_type.177 = bf16[2,256,4608]{1,0,2:T(2,128)(2,1)} reshape(bf16[512,8,576]{0,2,1:T(8,128)(2,1)} %convolution_convert_fusion.1) | data formatting | bytes 9437184 | tf_op jit(solution)/shard_map/convert_element_type | solution.py:85
  307.9 5.9 %fusion.81 = (bf16[2,256,1536]{1,0,2:T(2,128)(2,1)S(1)}, bf16[2,256,1536]{1,0,2:T(2,128)(2,1)}, bf16[2,256,1536]{1,0,2:T(2,128)(2,1)S(1)}) fusion(bf16[2,256,4608]{1,0,2:T(2,128)(2,1)} %convert_element_type.177), kind=kLoop, calls=%fused_computation.146 | loop fusion | bytes 9437184 | tf_op jit(solution)/shard_map/slice | solution.py:53
  313.8 1.4 copy.96
  315.2 3.6 copy.122
  318.9 1.7 copy.100
  320.6 0.4 multiply_reduce_fusion.2
  321.0 5.0 copy.121
  326.0 3.0 copy.98
  329.0 2.3 multiply_reduce_fusion.3
  331.4 0.5 multiply_multiply_fusion
  331.9 1.3 copy-done
  333.2 0.6 multiply_multiply_fusion.1
  333.9 0.5 subtract_convert_fusion.5
  334.5 0.5 subtract_convert_fusion.7
  335.0 2.8 fusion
  337.8 3.1 fusion.1
  341.0 3.2 fusion.38
  344.2 1.6 copy.102
  345.9 0.3 copy.123
  346.2 2.7 fusion.45
  348.9 2.8 copy.104
  351.7 6.3 %all-to-all-start.1 = ((bf16[2,256,1536]{2,0,1:T(2,128)(2,1)}), bf16[2,256,1536]{2,0,1:T(2,128)(2,1)S(1)}, u32[]{:S(2)}, u32[]{:S(2)}) async-start(bf16[2,256,1536]{2,0,1:T(2,128)(2,1)} %copy.104), calls=%async_computation.1 | async-start | bytes 3145728 | tf_op jit(solution)/shard_map/all_to_all | solution.py:243
  358.2 18.9 %copy.106 = bf16[8,576,1536]{2,1,0:T(8,128)(2,1)} copy(bf16[8,576,1536]{1,2,0:T(8,128)(2,1)} %bitcast.74) | data formatting | bytes 28311552 | tf_op jit(solution)/shard_map/tk,fkn->ftn/dot_general | solution.py:207
  377.1 8.0 %copy.117 = bf16[8,192,1536]{2,1,0:T(8,128)(2,1)} copy(bf16[8,192,1536]{1,2,0:T(8,128)(2,1)} %bitcast.78) | data formatting | bytes 9437184 | tf_op jit(solution)/shard_map/tk,fkn->ftn/dot_general | solution.py:207
  385.2 0.1 broadcast_or_fusion.1
  385.3 2.0 multiply_cosine_fusion.1
  387.3 8.4 %all-to-all-done.1 = bf16[2,256,1536]{2,0,1:T(2,128)(2,1)S(1)} async-done(((bf16[2,256,1536]{2,0,1:T(2,128)(2,1)}), bf16[2,256,1536]{2,0,1:T(2,128)(2,1)S(1)}, u32[]{:S(2)}, u32[]{:S(2)}) %all-to-all-start.1) | async-done | bytes 1572896 | tf_op jit(solution)/shard_map/all_to_all | solution.py:243
  395.7 2.1 copy.105
  397.9 1.1 bitcast_convert_fusion
  399.0 0.5 fusion.37
  399.5 0.6 fusion.36
  400.1 1.8 copy-done.1
  401.9 9.1 %convolution_convert_fusion = bf16[512,4608]{1,0:T(8,128)(2,1)} fusion(bf16[512,1536]{1,0:T(8,128)(2,1)S(1)} %bitcast.90, bf16[4608,1536]{1,0:T(8,128)(2,1)S(1)} %bitcast.75), kind=kOutput, calls=%fused_computation.6 | convolution fusion | flops 7250116608 | bytes 20447232 | tf_op jit(solution)/shard_map/tk,fkn->ftn/dot_general | solution.py:207
  411.0 5.5 %fusion.80 = (bf16[16,32,1536]{2,1,0:T(8,128)(2,1)}, f32[16,32,1536]{2,1,0:T(8,128)}, f32[16,32,1536]{2,1,0:T(8,128)S(1)}) fusion(bf16[16,32,4608]{2,1,0:T(8,128)(2,1)} %bitcast.80), kind=kLoop, calls=%fused_computation.145 | loop fusion | flops 1572864 | bytes 12582912 | tf_op jit(solution)/shard_map/slice | solution.py:54
  416.6 5.5 %reshape.265 = f32[16,32,24,64]{3,2,1,0:T(8,128)} reshape(f32[16,32,1536]{2,1,0:T(8,128)} %get-tuple-element.28) | data formatting | bytes 6291456 | tf_op jit(solution)/shard_map/convert_element_type | solution.py:53
  422.1 5.2 %multiply_reduce_fusion = f32[16,32,24]{2,1,0:T(8,128)} fusion(f32[16,32,24,64]{3,2,1,0:T(8,128)} %reshape.265), kind=kLoop, calls=%fused_computation.20 | loop fusion | flops 1560576 | bytes 3194880 | tf_op jit(solution)/shard_map/reduce_sum | solution.py:24
  427.3 1.7 copy.111
  429.0 1.6 add_rsqrt_fusion
  430.6 1.9 copy.112
  432.5 3.5 reshape.264
  436.0 4.5 multiply_reduce_fusion.1
  440.7 0.2 copy.109
  441.0 11.9 %fusion.6 = (f32[16,32,24,64]{3,0,2,1:T(8,128)S(1)}, f32[16,32,24,64]{3,0,2,1:T(8,128)S(1)}) fusion(f32[16,32,24,64]{3,2,1,0:T(8,128)} %reshape.265, f32[64]{0:T(128)S(1)} %get-tuple-element.45, f32[16,32,24]{0,2,1:T(8,128)S(1)} %copy-done.12, f32[64]{0:T(128)S(1)} %get-tuple-element.48, f32[16,32,24]{0,2,1:T(8,128)S(1)} %copy.109, ...), kind=kLoop, calls=%fused_computation.11 | loop fusion | flops 3145728 | bytes 12681728 | tf_op jit(solution)/shard_map/mul | solution.py:25
  453.0 8.0 %subtract_convert_fusion.1 = (bf16[16,32,24,16]{3,0,2,1:T(8,128)(2,1)}, bf16[16,32,24,16]{3,0,2,1:T(8,128)(2,1)}, bf16[16,32,24,16]{3,0,2,1:T(8,128)(2,1)}, bf16[16,32,24,16]{3,0,2,1:T(8,128)(2,1)}) fusion(f32[16,32,24,64]{3,0,2,1:T(8,128)S(1)} %get-tuple-element.65, f32[16,32,16]{2,0,1:T(8,128)S(1)} %copy-done.6, f32[16,32,16]{2,0,1:T(8,128)S(1)} %get-tuple-element.51, ...), kind=kLoop, calls=%fused_computation.19 | loop fusion | flops 3145728 | bytes 4849664 | tf_op jit(solution)/shard_map/convert.9
  461.0 7.7 %subtract_convert_fusion.3 = (bf16[16,32,24,16]{3,0,2,1:T(8,128)(2,1)}, bf16[16,32,24,16]{3,0,2,1:T(8,128)(2,1)}, bf16[16,32,24,16]{3,0,2,1:T(8,128)(2,1)}, bf16[16,32,24,16]{3,0,2,1:T(8,128)(2,1)}) fusion(f32[16,32,24,64]{3,0,2,1:T(8,128)S(1)} %get-tuple-element.66, f32[16,32,16]{2,0,1:T(8,128)S(1)} %copy-done.6, f32[16,32,16]{2,0,1:T(8,128)S(1)} %get-tuple-element.51, ...), kind=kLoop, calls=%fused_computation.24 | loop fusion | flops 3145728 | bytes 4849664 | tf_op jit(solution)/shard_map/convert.13
  468.7 5.2 %reshape.259 = bf16[16,32,24,64]{3,2,1,0:T(8,128)(2,1)} reshape(bf16[16,32,1536]{2,1,0:T(8,128)(2,1)} %get-tuple-element.27) | data formatting | bytes 3145728 | tf_op jit(solution)/shard_map/reshape | solution.py:54
  473.9 13.9 %fusion.12 = (f32[32,24,16]{2,1,0:T(8,128)S(1)}, f32[32,24,16,16]{2,3,1,0:T(8,128)S(1)}) fusion(pred[32,16,16]{1,2,0:T(8,128)(4,1)S(1)} %broadcast_or_fusion.1, bf16[16,32,24,16]{3,0,2,1:T(8,128)(2,1)} %get-tuple-element.23, bf16[16,32,24,16]{3,0,2,1:T(8,128)(2,1)} %get-tuple-element.24, bf16[16,32,24,16]{3,0,2,1:T(8,128)(2,1)} %get-tuple-element.16, ...), kind=kOutput, calls=%fused_computation.30 | convolution fusion | flops 38326272 | bytes 3989504 | tf_op jit(solution)/shard_map/lbhd,mbhd->bhlm/dot_general | solution.py:65
  487.8 2.7 fusion.13
  490.5 8.5 %fusion.5 = bf16[16,32,24,64]{3,0,2,1:T(8,128)(2,1)S(1)} fusion(f32[16,32,24]{0,2,1:T(8,128)S(1)} %bitcast.91, f32[32,24,16,16]{2,3,1,0:T(8,128)S(1)} %get-tuple-element.64, f32[32,24,16]{2,1,0:T(8,128)S(1)} %get-tuple-element.63, pred[32,16,16]{1,2,0:T(8,128)(4,1)S(1)} %broadcast_or_fusion.1, bf16[16,32,24,64]{3,2,1,0:T(8,128)(2,1)S(1)} %copy-done.5), kind=kOutput, calls=%fused_computation.9 | convolution fusion | flops 27525120 | bytes 4038656 | tf_op jit(solution)/shard_map/bhlm,mbhd->lbhd/dot_general | solution.py:73
  499.0 0.8 copy.116
  499.8 3.0 convert_element_type.204
  502.8 7.6 %fusion.44 = bf16[512,1536]{1,0:T(8,128)(2,1)} fusion(f32[512,1536]{1,0:T(8,128)} %bitcast.85, bf16[512,1536]{1,0:T(8,128)(2,1)} %convert_element_type.204, bf16[1536,1536]{1,0:T(8,128)(2,1)} %bitcast.84), kind=kOutput, calls=%fused_computation.72 | convolution fusion | flops 2417491968 | bytes 11010048 | tf_op jit(solution)/shard_map/tk,fkn->ftn/dot_general | solution.py:207
  (62 shorter events, 0.8 us)
Async XLA Ops:
  0.0 7.4 %copy-start.9 = (bf16[1536,576]{0,1:T(8,128)(2,1)S(1)}, bf16[1536,576]{0,1:T(8,128)(2,1)}, u32[]{:S(2)}) copy-start(bf16[1536,576]{0,1:T(8,128)(2,1)} %param.14) | copy-start | bytes 5308420
  0.0 281.8 %all-to-all-start = ((bf16[8,64,1536]{2,1,0:T(8,128)(2,1)}), bf16[8,64,1536]{2,1,0:T(8,128)(2,1)}, u32[]{:S(2)}, u32[]{:S(2)}) async-start(bf16[8,64,1536]{2,1,0:T(8,128)(2,1)} %bitcast.86), calls=%async_computation | async-start | bytes 3145728 | tf_op jit(solution)/shard_map/all_to_all | solution.py:223
  7.4 4.6 copy-start.10
  9.7 4.6 copy-start.13
  9.7 5.7 %copy-start.14 = (s32[4096]{0:T(1024)S(1)}, s32[4096]{0:T(1024)}, u32[]{:S(2)}) copy-start(s32[4096]{0:T(1024)} %param.10) | copy-start | bytes 49156
  273.3 8.0 %copy-start.16 = (s32[16,256]{1,0:T(8,128)S(1)}, s32[16,256]{1,0:T(8,128)}, u32[]{:S(2)}) copy-start(s32[16,256]{1,0:T(8,128)} %param.11) | copy-start | bytes 49156
  273.3 8.1 %copy-start.15 = (f32[2,1536]{1,0:T(2,128)S(1)}, f32[2,1536]{1,0:T(2,128)}, u32[]{:S(2)}) copy-start(f32[2,1536]{1,0:T(2,128)} %param.12) | copy-start | bytes 36868
  273.3 8.1 %copy-start.17 = (f32[2,2,64]{2,1,0:T(2,128)S(1)}, f32[2,2,64]{2,1,0:T(2,128)}, u32[]{:S(2)}) copy-start(f32[2,2,64]{2,1,0:T(2,128)} %param.13) | copy-start | bytes 3076
  286.3 13.9 %copy-start.3 = (bf16[512,1536]{1,0:T(8,128)(2,1)}, bf16[512,1536]{1,0:T(8,128)(2,1)S(1)}, u32[]{:S(2)}) copy-start(bf16[512,1536]{1,0:T(8,128)(2,1)S(1)} %scatter_custom_fusion) | copy-start | bytes 4718596
  331.4 1.9 copy-start
  337.8 3.2 copy-start.11
  340.9 5.3 %slice-start = ((s8[4718592]{0:T(1024)(128)(4,1)}), s8[4194304]{0:T(1024)(128)(4,1)S(1)}, s32[]{:S(2)}) async-start(s8[4718592]{0:T(1024)(128)(4,1)} %bitcast.81), calls=%async_computation.2 | async-start | bytes 8388608
  341.0 5.3 %slice-start.1 = ((s8[4718592]{0:T(1024)(128)(4,1)}), s8[524288]{0:T(1024)(128)(4,1)S(1)}, s32[]{:S(2)}) async-start(s8[4718592]{0:T(1024)(128)(4,1)} %bitcast.81), calls=%async_computation.3 | async-start | bytes 1048576
  344.2 2.0 copy-start.4
  351.7 44.1 %all-to-all-start.1 = ((bf16[2,256,1536]{2,0,1:T(2,128)(2,1)}), bf16[2,256,1536]{2,0,1:T(2,128)(2,1)S(1)}, u32[]{:S(2)}, u32[]{:S(2)}) async-start(bf16[2,256,1536]{2,0,1:T(2,128)(2,1)} %copy.104), calls=%async_computation.1 | async-start | bytes 3145728 | tf_op jit(solution)/shard_map/all_to_all | solution.py:243
  395.7 6.2 %copy-start.1 = (bf16[8,576,1536]{2,1,0:T(8,128)(2,1)S(1)}, bf16[8,576,1536]{2,1,0:T(8,128)(2,1)}, u32[]{:S(2)}) copy-start(bf16[8,576,1536]{2,1,0:T(8,128)(2,1)} %copy.106) | copy-start | bytes 42467332
  436.0 4.9 copy-start.12
  441.0 12.0 %copy-start.6 = (f32[16,32,16]{2,0,1:T(8,128)S(1)}, f32[16,32,16]{2,0,1:T(8,128)}, u32[]{:S(2)}) copy-start(f32[16,32,16]{2,0,1:T(8,128)} %get-tuple-element.52) | copy-start | bytes 98308
  441.0 12.0 %copy-start.7 = (f32[16,32,16]{2,0,1:T(8,128)S(1)}, f32[16,32,16]{2,0,1:T(8,128)}, u32[]{:S(2)}) copy-start(f32[16,32,16]{2,0,1:T(8,128)} %get-tuple-element.57) | copy-start | bytes 98308
  441.0 12.0 %copy-start.8 = (f32[16,32,16]{2,0,1:T(8,128)S(1)}, f32[16,32,16]{2,0,1:T(8,128)}, u32[]{:S(2)}) copy-start(f32[16,32,16]{2,0,1:T(8,128)} %get-tuple-element.58) | copy-start | bytes 98308
  468.7 5.2 %copy-start.2 = (bf16[16,32,24,16]{3,0,2,1:T(8,128)(2,1)S(1)}, bf16[16,32,24,16]{3,0,2,1:T(8,128)(2,1)}, u32[]{:S(2)}) copy-start(bf16[16,32,24,16]{3,0,2,1:T(8,128)(2,1)} %get-tuple-element.15) | copy-start | bytes 1179652
  487.8 2.7 copy-start.5

commit v2 on v1

--- a/solution.py
+++ b/solution.py
@@ -48,6 +48,8 @@
 def attend(qkv, gains, rows_pos, cols_pos, keys_live, column, heads):
     width = qkv.shape[-1] // 3
     size = width // heads
+    if fits(lax.axis_size("fsdp"), width) and size == 64:
+        return attend_pairs(qkv, gains, rows_pos, cols_pos, keys_live, column)
     shape = qkv.shape[:-1] + (heads, size)
     query = qkv[..., :width].reshape(shape).astype(jnp.float32)
     key = qkv[..., width : 2 * width].reshape(shape).astype(jnp.float32)
@@ -208,6 +210,92 @@
     return out.astype(jnp.float32).transpose(1, 0, 2).reshape(values.shape[0], -1)
 
 
+def attend_kernel(q_ref, k_ref, v_ref, bias_ref, cos_ref, sin_ref, gain_ref, o_ref):
+    shape = q_ref.shape
+    tokens = shape[0] * shape[1]
+    lane = lax.broadcasted_iota(jnp.int32, (tokens, 128), 1)
+    low = lane < 64
+    front = (lane % 32) < 16
+    cosine = cos_ref[...].reshape(tokens, 128)
+    sine = sin_ref[...].reshape(tokens, 128)
+    bias = bias_ref[0]
+
+    def prepare(ref, which):
+        t = ref[...].astype(jnp.float32).reshape(tokens, 128)
+        square = t * t
+        first = jnp.sum(jnp.where(low, square, 0.0), axis=1, keepdims=True)
+        second = jnp.sum(jnp.where(low, 0.0, square), axis=1, keepdims=True)
+        scale = lax.rsqrt(jnp.where(low, first, second) * (1.0 / 64.0) + EPS)
+        t = t * scale * gain_ref[pl.ds(which, 1), :]
+        partner = jnp.where(front, pltpu.roll(t, 112, 1), pltpu.roll(t, 16, 1))
+        return (t * cosine + partner * sine).astype(jnp.bfloat16)
+
+    query = prepare(q_ref, 0)
+    key = prepare(k_ref, 1)
+    value = v_ref[...].astype(jnp.float32).reshape(tokens, 128).astype(jnp.bfloat16)
+    mixed = []
+    for head in range(2):
+        own = low if head == 0 else ~low
+        one = jnp.where(own, query.astype(jnp.float32), 0.0).astype(jnp.bfloat16)
+        scores = lax.dot_general(
+            one, key, (((1,), (1,)), ((), ())), preferred_element_type=jnp.float32
+        )
+        scores = scores * 0.125 + bias
+        weights = jnp.exp(scores - jnp.max(scores, axis=1, keepdims=True))
+        total = jnp.sum(weights, axis=1, keepdims=True)
+        part = jnp.dot(weights.astype(jnp.bfloat16), value, preferred_element_type=jnp.float32)
+        mixed.append(part / total)
+    o_ref[...] = jnp.where(low, mixed[0], mixed[1]).reshape(shape).astype(jnp.bfloat16)
+
+
+def attend_pairs(qkv, gains, rows_pos, cols_pos, live, column):
+    lead, second, wide = qkv.shape
+    width = wide // 3
+    pairs = width // 128
+    quarter = 16
+    freq = 10000.0 ** (-jnp.arange(quarter).astype(jnp.float32) / quarter)
+    angles = [p.astype(jnp.float32)[..., None] * freq for p in (rows_pos, cols_pos)]
+    cosine = jnp.concatenate([jnp.cos(a) for a in angles for _ in range(2)], axis=-1)
+    sine = jnp.concatenate([v for a in angles for v in (-jnp.sin(a), jnp.sin(a))], axis=-1)
+    cosine = jnp.concatenate([cosine, cosine], axis=-1)
+    sine = jnp.concatenate([sine, sine], axis=-1)
+    gain = jnp.concatenate([gains, gains], axis=-1)
+    if column:
+        block = (lead, 16, 128)
+        groups, stride = second // 16, 16
+        alive = live.reshape(lead, groups, 16).transpose(1, 0, 2).reshape(groups, lead * 16)
+        place = lambda g, p: (0, g, p)
+    else:
+        block = (1, second, 128)
+        groups, stride = lead, 1
+        alive = live
+        place = lambda g, p: (g, 0, p)
+    tokens = block[0] * block[1]
+    at = jnp.arange(tokens)
+    same = (at[:, None] % stride) == (at[None, :] % stride)
+    allow = same[None] & ((alive[:, None, :] > 0) | (at[:, None] == at[None, :])[None])
+    bias = jnp.where(allow, 0.0, -1e30).astype(jnp.float32)
+    spec = lambda off: pl.BlockSpec(block, lambda g, p: place(g, p + off))
+    table = pl.BlockSpec(block, lambda g, p: place(g, 0))
+    return pl.pallas_call(
+        attend_kernel,
+        grid=(groups, pairs),
+        out_shape=jax.ShapeDtypeStruct((lead, second, width), jnp.bfloat16),
+        in_specs=[
+            spec(0),
+            spec(pairs),
+            spec(2 * pairs),
+            pl.BlockSpec((1, tokens, tokens), lambda g, p: (g, 0, 0)),
+            table,
+            table,
+            pl.BlockSpec((2, 128), lambda g, p: (0, 0)),
+        ],
+        out_specs=spec(0),
+        compiler_params=pltpu.CompilerParams(vmem_limit_bytes=32 * 1024 * 1024),
+        name="attend_column" if column else "attend_row",
+    )(qkv, qkv, qkv, bias, cosine, sine, gain)
+
+
 def on_device(tiles, tile_cell, tissue, norm_gain, qk_gain, row_qkv, row_out, col_qkv, col_out):
     count = lax.axis_size("fsdp")
     index = lax.axis_index("fsdp")

time: 518 us -> 460 us (0.89); the launches traced: 511 us -> 459 us
  Pallas kernels: 258 us -> 322 us
  other arithmetic: 60.7 us -> 4.78 us
  local copies, waits for them, and re-layouts: 108 us -> 77.9 us
  matrix products: 61.3 us -> 33.3 us
    pallas_call x0 -> x2, Pallas kernels: none -> 64.6 us  [attend_pairs(): pl.pallas_call(attend_kernel, grid=(groups, pairs), out_shape=jax.ShapeDt...]
    dot_general x4 -> x0, matrix products: 28.4 us -> none  [the longest x2 16.7 us: attend(): jnp.einsum(score_form, query, key, preferred_element_type=jnp.float32)]
    convert_element_type x7 -> x0, local copies, waits for them, and re-layouts: 19.1 us -> none  [the longest x2 7.17 us: attend(): key = qkv[..., width:2 * width].reshape(shape).astype(jnp.float32)]
    reduce_sum x6 -> x0, other arithmetic: 18.3 us -> none  [the longest x4 12.5 us: head_norm(): scale = lax.rsqrt(jnp.mean(values * values, axis=-1, keepdims=True) + EPS)]
    another operation x4 -> x0, other arithmetic: 16.8 us -> none
    mul x3 -> x0, other arithmetic: 13.1 us -> none  [head_norm(): return values * scale * gain]
    convert_element_type x1 -> x2, local copies, waits for them, and re-layouts: 7.69 us -> 20.1 us  [project_qkv(): return stacked(normed, weight).astype(jnp.bfloat16)]
    unnamed x47 -> x25, local copies, waits for them, and re-layouts: 20.2 us -> 10.4 us
  transfers between devices with their start and end apart: 2 -> 2, of which waited for: 1 -> 1; matrix products, arithmetic and copies ran while one was open for 9% -> 11% of each run, Pallas kernels for 50% -> 56%
where the time goes in v2:
time: 460 us; the launch traced here: 459 us
  Pallas kernels  322 us (70%)
  local copies, waits for them, and re-layouts  77.9 us (17%)
  matrix products  33.3 us (7%)
  starting transfers between devices  13.5 us (3%)
  waiting for transfers between devices  7.01 us (2%)
  other arithmetic  4.78 us (1%)
    pallas_call x1, Pallas kernels, gather(): pl.pallas_call(functools.partial(gather_kernel, n, part), out_shape=[jax....  257 us
    pallas_call x2, Pallas kernels, attend_pairs(): pl.pallas_call(attend_kernel, grid=(groups, pairs), out_shape=jax.ShapeDt...  64.6 us
    dot_general x3, local copies, waits for them, and re-layouts, stacked(): jnp.einsum('tk,fkn->ftn', values, weight, preferred_element_type=jnp.floa...  35 us
    dot_general x4, matrix products, stacked(): jnp.einsum('tk,fkn->ftn', values, weight, preferred_element_type=jnp.floa...  33.3 us
    convert_element_type x2, local copies, waits for them, and re-layouts, project_qkv(): return stacked(normed, weight).astype(jnp.bfloat16)  20.1 us
    unnamed x25, local copies, waits for them, and re-layouts  10.4 us
  transfers between devices with their start and end apart: 2, of which 1 were waited for; matrix products, arithmetic and copies ran while one was open for 11% of the time, Pallas kernels for 56%

profile of v2, /device:TPU:0, one launch (start us, length us, event | category | flops | bytes accessed | tf_op | source)
XLA Modules:
  0.0 458.7 jit_solution(11460160203157959950)
XLA Ops:
  0.0 0.0 copy-start.1
  0.0 7.4 %all-to-all-start = ((bf16[8,64,1536]{2,1,0:T(8,128)(2,1)}), bf16[8,64,1536]{2,1,0:T(8,128)(2,1)}, u32[]{:S(2)}, u32[]{:S(2)}) async-start(bf16[8,64,1536]{2,1,0:T(8,128)(2,1)} %bitcast.63), calls=%async_computation | async-start | bytes 3145728 | tf_op jit(solution)/shard_map/all_to_all | solution.py:311
  7.4 0.0 copy-start.2
  7.4 0.0 copy-done.1
  7.4 2.3 copy.60.refs_0_
  9.7 0.0 copy-start.3
  9.7 0.0 copy-start.4
  9.7 0.0 copy-start.6
  9.7 2.3 copy.61.refs_1_
  12.0 0.0 copy-done.2
  12.0 2.3 copy.62.refs_2_
  14.3 0.0 copy-done.3
  14.3 1.2 copy.63.refs_3_
  15.4 0.0 copy-done.4
  15.4 0.1 reshape.214
  15.5 0.1 sub.19
  15.6 0.0 copy-done.6
  15.6 0.1 constant_dynamic-slice_fusion
  15.7 0.1 copy.78
  15.8 0.1 copy.75
  15.9 0.1 gt.25
  16.0 257.3 %gather.1 = (bf16[8,1536,576]{2,1,0:T(8,128)(2,1)}, bf16[8,1536,192]{2,1,0:T(8,128)(2,1)}, bf16[8,1536,576]{2,1,0:T(8,128)(2,1)}, bf16[8,1536,192]{2,1,0:T(8,128)(2,1)}) custom-call(bf16[1536,576]{1,0:T(8,128)(2,1)} %copy.60.refs_0_, bf16[1536,192]{1,0:T(8,128)(2,1)} %copy.61.refs_1_, bf16[1536,576]{1,0:T(8,128)(2,1)} %copy.62.refs_2_, ...), custom_call_target="tpu_custom_call" | custom-call | tf_op jit(solution)/shard_map/gather/pallas_call | solution.py:195
  273.3 8.0 %copy.70 = bf16[8,192,1536]{2,1,0:T(8,128)(2,1)} copy(bf16[8,192,1536]{1,2,0:T(8,128)(2,1)} %bitcast.57) | data formatting | bytes 9437184 | tf_op jit(solution)/shard_map/tk,fkn->ftn/dot_general | solution.py:209
  281.3 0.0 copy-start.7
  281.3 0.0 copy-start.5
  281.3 0.6 multiply_sine_fusion.2
  281.9 0.8 concatenate.26.cos_ref
  282.7 0.8 concatenate.27.sin_ref
  283.6 0.0 copy-done.7
  283.6 0.1 pad_maximum_fusion
  283.7 0.0 copy-done.5
  283.7 0.1 iota_compare_fusion
  283.8 0.1 and_select_fusion
  284.0 0.0 all-to-all-done
  284.0 4.4 scatter_custom_fusion
  288.5 0.4 fusion
  288.8 13.5 %convolution_convert_fusion.1 = bf16[512,8,576]{0,2,1:T(8,128)(2,1)} fusion(bf16[8,1536,576]{2,1,0:T(8,128)(2,1)} %get-tuple-element.9, bf16[512,1536]{1,0:T(8,128)(2,1)S(1)} %scatter_custom_fusion, f32[1536]{0:T(1024)S(1)} %get-tuple-element.14, f32[512]{0:T(512)S(1)} %add_rsqrt_fusion.1), kind=kOutput, calls=%fused_computation.16 | convolution fusion | flops 7253262336 | bytes 20455424 | tf_op jit(solution)/shard_map/tk,fkn->ftn/dot_general | solution.py:209
  302.3 7.7 %convert_element_type.123 = bf16[2,256,4608]{1,0,2:T(2,128)(2,1)} reshape(bf16[512,8,576]{0,2,1:T(8,128)(2,1)} %convolution_convert_fusion.1) | data formatting | bytes 9437184 | tf_op jit(solution)/shard_map/convert_element_type | solution.py:87
  310.0 12.5 %copy.67.q_ref.k_ref.v_ref = bf16[2,256,4608]{2,1,0:T(8,128)(2,1)} copy(bf16[2,256,4608]{1,0,2:T(2,128)(2,1)} %convert_element_type.123) | data formatting | bytes 9437184 | tf_op jit(solution)/shard_map/convert_element_type | solution.py:87
  322.4 0.0 copy-start
  322.4 2.3 copy-done
  324.8 32.1 %attend_row.1 = bf16[2,256,1536]{2,1,0:T(8,128)(2,1)S(1)} custom-call(bf16[2,256,4608]{2,1,0:T(8,128)(2,1)S(1)} %copy-done, bf16[2,256,4608]{2,1,0:T(8,128)(2,1)S(1)} %copy-done, bf16[2,256,4608]{2,1,0:T(8,128)(2,1)S(1)} %copy-done, f32[2,256,256]{2,1,0:T(8,128)S(1)} %get-tuple-element.16.bias_ref, f32[2,256,128]{2,1,0:T(8,128)S(1)} %concatenate.26.cos_ref, ...), custom_call_target="tpu_custom_call" | custom-call | tf_op jit(solution)/shard_map/attend_row/pallas_call | solution.py:280
  356.9 5.0 %fusion.7 = bf16[512,1536]{1,0:T(8,128)(2,1)S(1)} fusion(bf16[512,1536]{1,0:T(8,128)(2,1)S(1)} %bitcast.51, bf16[1536,1536]{1,0:T(8,128)(2,1)} %bitcast.58, bf16[512,1536]{1,0:T(8,128)(2,1)S(1)} %scatter_custom_fusion), kind=kOutput, calls=%fused_computation.15 | convolution fusion | flops 2418278400 | bytes 9437184 | tf_op jit(solution)/shard_map/tk,fkn->ftn/dot_general | solution.py:209
  361.9 2.8 copy.71
  364.7 6.1 %all-to-all-start.1 = ((bf16[2,256,1536]{2,0,1:T(2,128)(2,1)}), bf16[2,256,1536]{2,0,1:T(2,128)(2,1)S(1)}, u32[]{:S(2)}, u32[]{:S(2)}) async-start(bf16[2,256,1536]{2,0,1:T(2,128)(2,1)} %copy.71), calls=%async_computation.1 | async-start | bytes 3145728 | tf_op jit(solution)/shard_map/all_to_all | solution.py:331
  370.8 19.0 %copy.73 = bf16[8,576,1536]{2,1,0:T(8,128)(2,1)} copy(bf16[8,576,1536]{1,2,0:T(8,128)(2,1)} %bitcast.53) | data formatting | bytes 28311552 | tf_op jit(solution)/shard_map/tk,fkn->ftn/dot_general | solution.py:209
  389.8 8.0 %copy.76 = bf16[8,192,1536]{2,1,0:T(8,128)(2,1)} copy(bf16[8,192,1536]{1,2,0:T(8,128)(2,1)} %bitcast.56) | data formatting | bytes 9437184 | tf_op jit(solution)/shard_map/tk,fkn->ftn/dot_general | solution.py:209
  397.8 1.2 multiply_sine_fusion
  399.0 0.8 concatenate.29.cos_ref
  399.8 1.8 concatenate.30.sin_ref
  401.6 7.0 %all-to-all-done.1 = bf16[2,256,1536]{2,0,1:T(2,128)(2,1)S(1)} async-done(((bf16[2,256,1536]{2,0,1:T(2,128)(2,1)}), bf16[2,256,1536]{2,0,1:T(2,128)(2,1)S(1)}, u32[]{:S(2)}, u32[]{:S(2)}) %all-to-all-start.1) | async-done | bytes 1572896 | tf_op jit(solution)/shard_map/all_to_all | solution.py:331
  408.6 0.5 copy.72
  409.0 1.1 bitcast_convert_fusion
  410.1 0.5 fusion.5
  410.6 0.0 slice-start
  410.7 0.6 fusion.4
  411.3 0.0 slice-start.1
  411.3 11.1 %convolution_convert_fusion = bf16[512,4608]{1,0:T(8,128)(2,1)S(1)} fusion(bf16[512,1536]{1,0:T(8,128)(2,1)S(1)} %bitcast.65, bf16[4608,1536]{1,0:T(8,128)(2,1)} %bitcast.54), kind=kOutput, calls=%fused_computation.1 | convolution fusion | flops 7250116608 | bytes 20447232 | tf_op jit(solution)/shard_map/tk,fkn->ftn/dot_general | solution.py:209
  422.4 32.5 %attend_column.1 = bf16[16,32,1536]{2,1,0:T(8,128)(2,1)S(1)} custom-call(bf16[16,32,4608]{2,1,0:T(8,128)(2,1)S(1)} %bitcast.48, bf16[16,32,4608]{2,1,0:T(8,128)(2,1)S(1)} %bitcast.49, bf16[16,32,4608]{2,1,0:T(8,128)(2,1)S(1)} %bitcast.50, f32[2,256,256]{2,1,0:T(8,128)S(1)} %get-tuple-element.15.bias_ref, f32[16,32,128]{2,1,0:T(8,128)S(1)} %concatenate.29.cos_ref, ...), custom_call_target="tpu_custom_call" | custom-call | tf_op jit(solution)/shard_map/attend_column/pallas_call | solution.py:280
  454.9 0.0 slice-done
  454.9 0.0 slice-done.1
  454.9 3.7 fusion.6
  (15 shorter events, 0.1 us)
Async XLA Ops:
  0.0 7.4 %copy-start.1 = (bf16[1536,576]{0,1:T(8,128)(2,1)S(1)}, bf16[1536,576]{0,1:T(8,128)(2,1)}, u32[]{:S(2)}) copy-start(bf16[1536,576]{0,1:T(8,128)(2,1)} %param.14) | copy-start | bytes 5308420
  0.0 284.0 %all-to-all-start = ((bf16[8,64,1536]{2,1,0:T(8,128)(2,1)}), bf16[8,64,1536]{2,1,0:T(8,128)(2,1)}, u32[]{:S(2)}, u32[]{:S(2)}) async-start(bf16[8,64,1536]{2,1,0:T(8,128)(2,1)} %bitcast.63), calls=%async_computation | async-start | bytes 3145728 | tf_op jit(solution)/shard_map/all_to_all | solution.py:311
  7.4 4.6 copy-start.2
  9.7 4.6 copy-start.3
  9.7 5.7 %copy-start.4 = (s32[4096]{0:T(1024)S(1)}, s32[4096]{0:T(1024)}, u32[]{:S(2)}) copy-start(s32[4096]{0:T(1024)} %param.10) | copy-start | bytes 49156
  9.7 5.9 %copy-start.6 = (s32[16,256]{1,0:T(8,128)S(1)}, s32[16,256]{1,0:T(8,128)}, u32[]{:S(2)}) copy-start(s32[16,256]{1,0:T(8,128)} %param.11) | copy-start | bytes 49156
  281.3 2.3 copy-start.7
  281.3 2.4 copy-start.5
  322.4 2.3 copy-start
  364.7 43.9 %all-to-all-start.1 = ((bf16[2,256,1536]{2,0,1:T(2,128)(2,1)}), bf16[2,256,1536]{2,0,1:T(2,128)(2,1)S(1)}, u32[]{:S(2)}, u32[]{:S(2)}) async-start(bf16[2,256,1536]{2,0,1:T(2,128)(2,1)} %copy.71), calls=%async_computation.1 | async-start | bytes 3145728 | tf_op jit(solution)/shard_map/all_to_all | solution.py:331
  410.6 44.3 %slice-start = ((s8[4718592]{0:T(1024)(128)(4,1)}), s8[4194304]{0:T(1024)(128)(4,1)S(1)}, s32[]{:S(2)}) async-start(s8[4718592]{0:T(1024)(128)(4,1)} %bitcast.59), calls=%async_computation.2 | async-start | bytes 8388608
  411.3 43.7 %slice-start.1 = ((s8[4718592]{0:T(1024)(128)(4,1)}), s8[524288]{0:T(1024)(128)(4,1)S(1)}, s32[]{:S(2)}) async-start(s8[4718592]{0:T(1024)(128)(4,1)} %bitcast.59), calls=%async_computation.3 | async-start | bytes 1048576
